TPU v7x, 32 devices: a whole 2x2x4 slice. The times are simulated.
32 devices in a mesh: wide: 8 (over z, y), narrow: 4 (over x, core).
Axes of the slice: x: 2, y: 2, z: 4, core: 2. Of those that a mesh axis runs over, the one named last changes fastest.
Arguments:
- features: bfloat16 [8, 4, 128, 128], P('wide', 'narrow'), may hold values from -6 to 6
- offsets: bfloat16 [8, 4, 2, 128], P('wide', 'narrow'), may hold values from 0 to 1
- counts: int32 [8, 4], P('wide', 'narrow'), may hold values from 64 to 128
- owned_pairs: int32 [8, 4, 8], P('wide', 'narrow'), may hold values from 0 to 1, as said below
- kernels: bfloat16 [8, 128, 128], replicated, may hold values from -0.1875 to 0.1875
- cotangent: bfloat16 [8, 4, 128, 128], P('wide', 'narrow'), may hold values from -6 to 6
Outputs:
- corrected: bfloat16 [8, 4, 128, 128], P('wide', 'narrow')
- grad_features: float32 [8, 4, 128, 128], P('wide', 'narrow')
- grad_kernels: float32 [8, 128, 128], replicated
Inputs may be any that keep to these rules, and one draw needn't show every extreme that they name: owned_pairs[x, y, s] = 1 means that the device of cell (x, y) evaluates the pair of tower cell (x, y + a) and plate cell (x + b, y), indices modulo 8 and 4, with (a, b) the s-th of (0,1), (0,-1), (-1,0), (1,0), (-1,1), (1,-1), (1,1), (-1,-1). Each unordered pair of distinct cells whose indices differ by at most one in each dimension is evaluated at most once, by one of its two candidate devices. Some device evaluates all 8.
All inputs are finite; a program needn't handle non-finite values.
Results may differ from a plain program's by a relative error of at most 0.0075.
Values may be sent and summed in bfloat16 or wider, within the bound.
A program may use at most 64 MiB of HBM per device.

v0:
```python
import math

import jax
import jax.numpy as jnp
from jax import lax
from jax.experimental import pallas as pl
from jax.experimental.pallas import tpu as pltpu
from jax.sharding import PartitionSpec as P

KERNEL_SCALE = 0.0625
SLOT_SHIFTS = ((0, 1), (0, -1), (-1, 0), (1, 0), (-1, 1), (1, -1), (1, 1), (-1, -1))
AROUND = ((0, 0), (-1, 0), (1, 0), (0, -1), (0, 1), (-1, -1), (-1, 1), (1, -1), (1, 1))
NEAR = 5
FLAGS = 8
CHUNK = 32
VMEM_BYTES = 56 * 1024 * 1024
F32 = jnp.float32
BF16 = jnp.bfloat16


def spot(dx, dy):
    return AROUND.index((dx, dy))


def make_kernel(nw, nn, particles, channels, levels):
    rows = levels * channels
    rows_n = rows // nn
    rows_w = rows_n // nw
    scattered = rows_w % 16 == 0 and rows_w > 0
    norm = 1.0 / math.sqrt(nw * nn * particles)
    near = NEAR * particles
    gathered = (nn, nw, rows_w, channels) if scattered else (nn, 1, rows_n, channels)
    far_first = sorted(range(1, nn), key=lambda d: -min(d, nn - d))

    def kernel(
        counts_ref, owned_ref, feat_ref, off_ref, kern_ref, cot_ref,
        corrected_ref, grad_ref, n_out,
        f_all, g_all, k_all, geo, rows_of, s_all, f_acc, own_x, own_y, own_live, z_all,
        force_out, grad_out, w_part, n_in, w_sum, w_in, w_out,
        in_sem, out_sem, f_send, f_recv, g_send, g_recv, p_send, p_recv,
        ns_send, ns_recv, ws_send, ws_recv, wa_send, wa_recv, na_send, na_recv,
    ):
        mw = lax.axis_index("wide")
        mn = lax.axis_index("narrow")

        def wide_peer(step):
            return (lax.rem(mw + step + nw, nw), mn)

        def narrow_peer(step):
            return (mw, lax.rem(mn + step + nn, nn))

        barrier = pltpu.get_barrier_semaphore()
        for d in range(1, nw):
            pl.semaphore_signal(
                barrier, inc=1, device_id=wide_peer(d), device_id_type=pl.DeviceIdType.MESH
            )
        for d in range(1, nn):
            pl.semaphore_signal(
                barrier, inc=1, device_id=narrow_peer(d), device_id_type=pl.DeviceIdType.MESH
            )

        def remote(src, dst, send, recv, peer):
            return pltpu.make_async_remote_copy(
                src_ref=src, dst_ref=dst, send_sem=send, recv_sem=recv,
                device_id=peer, device_id_type=pl.DeviceIdType.MESH,
            )

        def block(ref, q):
            return ref.at[pl.ds(q * particles, particles)]

        feat_in = pltpu.make_async_copy(feat_ref.at[0, 0], block(f_all, 0), in_sem.at[0])
        cot_in = pltpu.make_async_copy(cot_ref.at[0, 0], block(g_all, 0), in_sem.at[1])
        kern_in = pltpu.make_async_copy(kern_ref, k_all, in_sem.at[2])
        feat_in.start()
        cot_in.start()
        kern_in.start()

        off = off_ref[0, 0].astype(F32)
        lane = lax.broadcasted_iota(jnp.int32, (1, particles), 1)
        live = (lane < counts_ref[0, 0]).astype(F32)
        geo[0, 0:2, :] = off
        geo[0, 2:3, :] = live
        for s in range(len(SLOT_SHIFTS)):
            geo[0, FLAGS + s : FLAGS + s + 1, :] = jnp.full(
                (1, particles), owned_ref[0, 0, s].astype(F32)
            )

        pl.semaphore_wait(barrier, nw - 1 + nn - 1)

        geo_copies, f_copies, g_copies = {}, {}, {}

        def send_geo(src, slot, peer):
            copy = remote(geo.at[src], geo.at[slot], p_send.at[slot], p_recv.at[slot], peer)
            copy.start()
            geo_copies[slot] = copy

        def send_f(src, slot, peer):
            copy = remote(
                block(f_all, src), block(f_all, slot), f_send.at[slot], f_recv.at[slot], peer
            )
            copy.start()
            f_copies[slot] = copy

        def send_g(src, slot, peer):
            copy = remote(
                block(g_all, src), block(g_all, slot), g_send.at[slot], g_recv.at[slot], peer
            )
            copy.start()
            g_copies[slot] = copy

        def forward(send, copies):
            for dx in (1, -1):
                copies[spot(dx, 0)].wait_recv()
                for d in (1, -1):
                    send(spot(dx, 0), spot(dx, -d), narrow_peer(d))

        own_sends = [(spot(-d, 0), wide_peer(d)) for d in (1, -1)]
        own_sends += [(spot(0, -d), narrow_peer(d)) for d in (1, -1)]
        for slot, peer in own_sends:
            send_geo(0, slot, peer)
        feat_in.wait()
        for slot, peer in own_sends:
            send_f(0, slot, peer)
        cot_in.wait()
        for slot, peer in own_sends:
            send_g(0, slot, peer)

        own_x[...] = jnp.broadcast_to(off[0:1], (particles, particles)).T
        own_y[...] = jnp.broadcast_to(off[1:2], (particles, particles)).T
        own_live[...] = jnp.broadcast_to(live, (particles, particles)).T

        def pair_rows(q):
            dx, dy = AROUND[q]
            there = geo[q]
            weight = there[2:3] * KERNEL_SCALE
            if q == 0:
                weight = weight * 2.0
            else:
                first = FLAGS + SLOT_SHIFTS.index((-dy, dx))
                second = FLAGS + SLOT_SHIFTS.index((dy, -dx))
                weight = weight * (
                    geo[spot(0, dy), first : first + 1] + geo[spot(dx, 0), second : second + 1]
                )
            rows_of[q, 0:1, :] = there[0:1] + float(dx)
            rows_of[q, 1:2, :] = there[1:2] + float(dy)
            rows_of[q, 2:3, :] = weight

        def pair_kernels(start, stop):
            for q in range(start, stop):
                pair_rows(q)
            chunks = particles // CHUNK

            @pl.loop(start * chunks, stop * chunks)
            def _(step):
                q = step // chunks
                r = pl.multiple_of(step % chunks * CHUNK, CHUNK)
                lanes = pl.ds(pl.multiple_of(q * particles, particles), particles)
                u = rows_of[q, 0:1, :] - own_x[pl.ds(r, CHUNK), :]
                v = rows_of[q, 1:2, :] - own_y[pl.ds(r, CHUNK), :]
                square = u * u + v * v
                triple = 3.0 * jnp.sqrt(square)
                window = jnp.maximum(1.0 - square, 0.0)
                window = window * window * rows_of[q, 2:3, :]
                wu = window * u
                wv = window * v
                for level in range(levels // 2):
                    bump = jnp.maximum(1.0 - jnp.abs(triple - float(level)), 0.0)
                    for part, value in ((0, wu), (1, wv)):
                        base = (2 * level + part) * particles
                        s_all[pl.ds(base + r, CHUNK), lanes] = (bump * value).astype(BF16)

        pair_kernels(0, 1)
        forward(send_geo, geo_copies)
        for dy in (1, -1):
            geo_copies[spot(0, dy)].wait_recv()
        pair_kernels(1, NEAR)
        forward(send_f, f_copies)
        for q in range(NEAR, len(AROUND)):
            geo_copies[q].wait_recv()
        pair_kernels(NEAR, len(AROUND))
        forward(send_g, g_copies)
        for dy in (1, -1):
            f_copies[spot(0, dy)].wait_recv()

        def with_ones(blocks):
            return jnp.concatenate([blocks, jnp.ones(blocks.shape, BF16)], axis=1)

        @pl.loop(0, levels // 2)
        def _(step):
            span = pl.ds(pl.multiple_of(step * 2 * particles, 2 * particles), 2 * particles)
            f_acc[span, :] = jnp.dot(
                s_all[span, 0:near], with_ones(f_all[0:near, :]), preferred_element_type=F32
            )

        for q in range(NEAR, len(AROUND)):
            f_copies[q].wait_recv()

        def finish_z(level, count):
            span = pl.ds(pl.multiple_of(level * particles, particles), count * particles)
            acc = f_acc[span, :] + jnp.dot(
                s_all[span, near:], with_ones(f_all[near:, :]), preferred_element_type=F32
            )
            f_acc[span, channels:] = acc[:, channels:]
            feat = f_all[0:particles, :].astype(F32)
            parts = []
            for j in range(count):
                mine = acc[j * particles : (j + 1) * particles]
                z = ((mine[:, channels:] * feat + mine[:, 0:channels]) * own_live[...]).astype(BF16)
                z_all[level + j] = z
                parts.append(
                    lax.dot_general(
                        z, g_all[0:particles, :], (((0,), (0,)), ((), ())),
                        preferred_element_type=F32,
                    ).astype(BF16)
                )
            return jnp.concatenate(parts, axis=0)

        def part_copy(d):
            peer = narrow_peer(d)
            return remote(
                w_part.at[peer[1]], n_in.at[d - 1], ns_send.at[d - 1], ns_recv.at[d - 1], peer
            )

        if levels % nn == 0:
            each = levels // nn

            @pl.loop(1, nn + 1)
            def _(d):
                piece = narrow_peer(d)[1]
                w_part[piece] = finish_z(piece * each, each)

                @pl.when(d < nn)
                def _():
                    part_copy(d).start()
        else:
            split = nn // levels
            assert split * levels == nn

            @pl.loop(0, levels)
            def _(level):
                part = finish_z(level, 1)
                for j in range(split):
                    w_part[level * split + j] = part[j * rows_n : (j + 1) * rows_n]

            @pl.loop(1, nn)
            def _(d):
                part_copy(d).start()

        kern_in.wait()
        for dy in (1, -1):
            g_copies[spot(0, dy)].wait_recv()
        for q in range(NEAR, len(AROUND)):
            g_copies[q].wait_recv()
        force_out[...] = jnp.zeros_like(force_out)
        grad_out[...] = jnp.zeros_like(grad_out)

        @pl.loop(0, levels)
        def _(k):
            span = pl.ds(pl.multiple_of(k * particles, particles), particles)
            force_out[...] += jnp.dot(z_all[k], k_all[k], preferred_element_type=F32)
            acc = jnp.dot(s_all[span, :], g_all[...], preferred_element_type=F32)
            own = f_acc[span, channels:] * g_all[0:particles, :].astype(F32)
            y = ((own - acc) * own_live[...]).astype(BF16)
            grad_out[...] += lax.dot_general(
                y, k_all[k], (((1,), (1,)), ((), ())), preferred_element_type=F32
            )

        corrected_out = f_all.at[pl.ds(0, particles)]
        for copies in (f_copies, g_copies, geo_copies):
            for copy in copies.values():
                copy.wait_send()
        corrected_out[...] = force_out[...].astype(BF16)
        force_copy = pltpu.make_async_copy(corrected_out, corrected_ref.at[0, 0], out_sem.at[0])
        grad_copy = pltpu.make_async_copy(grad_out, grad_ref.at[0, 0], out_sem.at[1])
        force_copy.start()
        grad_copy.start()

        total = w_part[mn].astype(F32)
        for d in range(1, nn):
            part_copy(d).wait_recv()
            total += n_in[d - 1].astype(F32)

        def row_copy(d, step):
            at = lax.rem(mw - step + nw, nw) if scattered else 0
            return remote(
                w_out.at[at], n_out.at[mn, at],
                na_send.at[d - 1, step], na_recv.at[d - 1, step], narrow_peer(d),
            )

        def send_row(step):
            for d in far_first:
                row_copy(d, step).start()

        if scattered:

            def scatter_copy(d):
                peer = wide_peer(d)
                return remote(
                    w_sum.at[peer[0]], w_in.at[d - 1], ws_send.at[d - 1], ws_recv.at[d - 1], peer
                )

            def column_copy(d):
                return remote(
                    w_out.at[mw], w_out.at[mw],
                    wa_send.at[d - 1], wa_recv.at[d - 1], wide_peer(d),
                )

            w_sum[...] = total.astype(BF16).reshape(nw, rows_w, channels)
            for d in range(1, nw):
                scatter_copy(d).start()
            piece = w_sum[mw].astype(F32)
            for d in range(1, nw):
                scatter_copy(d).wait_recv()
                piece += w_in[d - 1].astype(F32)
            w_out[mw] = (piece * norm).astype(BF16)
            for d in range(1, nw):
                column_copy(d).start()
            send_row(0)

            @pl.loop(1, nw)
            def _(step):
                column_copy(step).wait_recv()
                send_row(step)

            @pl.loop(1, nw)
            def _(d):
                scatter_copy(d).wait_send()
                column_copy(d).wait_send()
        else:

            def scatter_copy(d):
                return remote(
                    w_in.at[mw], w_in.at[mw], ws_send.at[d - 1], ws_recv.at[d - 1], wide_peer(d)
                )

            w_in[mw] = total.astype(BF16)

            @pl.loop(1, nw)
            def _(d):
                scatter_copy(d).start()

            @pl.loop(1, nw)
            def _(d):
                scatter_copy(d).wait()

            w_out[0] = (jnp.sum(w_in[...].astype(F32), axis=0) * norm).astype(BF16)
            send_row(0)
        own_copy = pltpu.make_async_copy(w_out, n_out.at[mn], out_sem.at[2])
        own_copy.start()

        @pl.loop(1, nn)
        def _(d):
            part_copy(d).wait_send()

        @pl.loop(0, gathered[1])
        def _(step):
            for d in range(1, nn):
                row_copy(d, step).wait()

        force_copy.wait()
        grad_copy.wait()
        own_copy.wait()

    spots = len(AROUND)
    wide_in = (nw - 1, rows_w, channels) if scattered else (nw, rows_n, channels)
    wide_sum = (nw, rows_w, channels) if scattered else (1, 16, channels)
    dma = pltpu.SemaphoreType.DMA
    square = pltpu.VMEM((particles, particles), F32)
    block_sum = pltpu.VMEM((particles, channels), F32)
    scratch = [
        pltpu.VMEM((spots * particles, channels), BF16),
        pltpu.VMEM((spots * particles, channels), BF16),
        pltpu.VMEM((levels, channels, channels), BF16),
        pltpu.VMEM((spots, FLAGS + len(SLOT_SHIFTS), particles), F32),
        pltpu.VMEM((spots, FLAGS, particles), F32),
        pltpu.VMEM((levels * particles, spots * particles), BF16),
        pltpu.VMEM((levels * particles, 2 * channels), F32),
        square, square, square,
        pltpu.VMEM((levels, particles, channels), BF16),
        block_sum, block_sum,
        pltpu.VMEM((nn, rows_n, channels), BF16),
        pltpu.VMEM((nn - 1, rows_n, channels), BF16),
        pltpu.VMEM(wide_sum, BF16),
        pltpu.VMEM(wide_in, BF16),
        pltpu.VMEM(gathered[1:], BF16),
        dma((3,)), dma((3,)),
        dma((spots,)), dma((spots,)), dma((spots,)), dma((spots,)), dma((spots,)), dma((spots,)),
        dma((nn - 1,)), dma((nn - 1,)), dma((nw - 1,)), dma((nw - 1,)),
        dma((nw - 1,)), dma((nw - 1,)),
        dma((nn - 1, gathered[1])), dma((nn - 1, gathered[1])),
    ]
    return kernel, scratch, gathered


def deliver(
    corrected_in, grad_in, weights_in, corrected_ref, grad_ref, weights_ref, narrow, wide, sems
):
    load = pltpu.make_async_copy(weights_in, narrow, sems.at[0])
    copies = [
        pltpu.make_async_copy(grad_in, grad_ref, sems.at[1]),
        pltpu.make_async_copy(corrected_in, corrected_ref, sems.at[2]),
        pltpu.make_async_copy(wide, weights_ref, sems.at[3]),
    ]
    load.start()
    copies[0].start()
    copies[1].start()
    load.wait()
    wide[...] = narrow[...].astype(F32).reshape(wide.shape)
    copies[2].start()
    for copy in copies:
        copy.wait()


def body(features, offsets, counts, owned_pairs, kernels, cotangent):
    particles, channels = features.shape[2:]
    levels = kernels.shape[0]
    nw, nn = lax.axis_size("wide"), lax.axis_size("narrow")
    kernel, scratch, gathered = make_kernel(nw, nn, particles, channels, levels)
    vmem = pl.BlockSpec(memory_space=pltpu.VMEM)
    smem = pl.BlockSpec(memory_space=pltpu.SMEM)
    hbm = pl.BlockSpec(memory_space=pltpu.HBM)
    outs = (
        jax.ShapeDtypeStruct(features.shape, BF16),
        jax.ShapeDtypeStruct(features.shape, F32),
    )
    results = pl.pallas_call(
        kernel,
        out_shape=outs + (jax.ShapeDtypeStruct(gathered, BF16),),
        in_specs=[smem, smem, hbm, vmem, hbm, hbm],
        out_specs=(hbm, hbm, hbm),
        scratch_shapes=scratch,
        compiler_params=pltpu.CompilerParams(
            collective_id=0, has_side_effects=True, vmem_limit_bytes=VMEM_BYTES
        ),
        name="antisymmetric_convolution",
    )(counts, owned_pairs, features, offsets, kernels, cotangent)
    return pl.pallas_call(
        deliver,
        out_shape=outs + (jax.ShapeDtypeStruct(kernels.shape, F32),),
        in_specs=[hbm, hbm, hbm],
        out_specs=(hbm, hbm, hbm),
        scratch_shapes=[
            pltpu.VMEM(gathered, BF16),
            pltpu.VMEM(kernels.shape, F32),
            pltpu.SemaphoreType.DMA((4,)),
        ],
        compiler_params=pltpu.CompilerParams(vmem_limit_bytes=VMEM_BYTES),
        name="deliver",
    )(*results)


def solution(mesh):
    placed = (
        P("wide", "narrow", None, None),
        P("wide", "narrow", None, None),
        P("wide", "narrow"),
        P("wide", "narrow", None),
        P(),
        P("wide", "narrow", None, None),
    )
    return jax.shard_map(
        body,
        mesh=mesh,
        in_specs=placed,
        out_specs=(P("wide", "narrow", None, None), P("wide", "narrow", None, None), P()),
        check_vma=False,
    )
```

profile of v0, /device:TPU:0, one launch (start us, length us, event | category | flops | bytes accessed | tf_op | source)
XLA Modules:
  0.0 38.7 jit_solution(11898972885999013866)
XLA Ops:
  1.3 33.3 %antisymmetric_convolution.1 = (bf16[1,1,128,128]{3,2,1,0:T(8,128)(2,1)}, f32[1,1,128,128]{3,2,1,0:T(8,128)}, bf16[4,8,32,128]{3,2,1,0:T(8,128)(2,1)}) custom-call(s32[1,1]{1,0:T(1,128)S(6)} %copy.9.counts_ref, s32[1,1,8]{2,1,0:T(1,128)} %owned_ref.1, bf16[1,1,128,128]{3,2,1,0:T(8,128)(2,1)} %feat_ref.1, bf16[1,1,2,128]{3,2,1,0:T(2,128)(2,1)} %off_ref.1, ...), custom_call_target="tpu_custom_call" | custom-call | tf_op jit(solution)/shard_map/antisymmetric_convolution/pallas_call | solution.py:426
  34.5 4.1 %deliver.1 = (bf16[1,1,128,128]{3,2,1,0:T(8,128)(2,1)}, f32[1,1,128,128]{3,2,1,0:T(8,128)}, f32[8,128,128]{2,1,0:T(8,128)}) custom-call(bf16[1,1,128,128]{3,2,1,0:T(8,128)(2,1)} %get-tuple-element.6.corrected_in, f32[1,1,128,128]{3,2,1,0:T(8,128)} %get-tuple-element.7.grad_in, bf16[4,8,32,128]{3,2,1,0:T(8,128)(2,1)} %get-tuple-element.8.weights_in), custom_call_target="tpu_custom_call" | custom-call | tf_op jit(solution)/shard_map/deliver/pallas_call | solution.py:437
where the time goes:
time: 38.8 us; the launch traced here: 38.7 us
  Pallas kernels  37.4 us (96%)
  between operations  1.28 us (3%)
    pallas_call x1, Pallas kernels, body(): pl.pallas_call(kernel, out_shape=outs + (jax.ShapeDtypeStruct(gathered, B...  33.3 us
    pallas_call x1, Pallas kernels, body(): pl.pallas_call(deliver, out_shape=outs + (jax.ShapeDtypeStruct(kernels.sh...  4.12 us

commit v1 on v0

--- a/solution.py
+++ b/solution.py
@@ -12,7 +12,8 @@
 AROUND = ((0, 0), (-1, 0), (1, 0), (0, -1), (0, 1), (-1, -1), (-1, 1), (1, -1), (1, 1))
 NEAR = 5
 FLAGS = 8
-CHUNK = 32
+CHUNK = 64
+TINY = 1e-30
 VMEM_BYTES = 56 * 1024 * 1024
 F32 = jnp.float32
 BF16 = jnp.bfloat16
@@ -158,7 +159,7 @@
                 u = rows_of[q, 0:1, :] - own_x[pl.ds(r, CHUNK), :]
                 v = rows_of[q, 1:2, :] - own_y[pl.ds(r, CHUNK), :]
                 square = u * u + v * v
-                triple = 3.0 * jnp.sqrt(square)
+                triple = 3.0 * (square * lax.rsqrt(jnp.maximum(square, TINY)))
                 window = jnp.maximum(1.0 - square, 0.0)
                 window = window * window * rows_of[q, 2:3, :]
                 wu = window * u
@@ -254,8 +255,7 @@
         force_out[...] = jnp.zeros_like(force_out)
         grad_out[...] = jnp.zeros_like(grad_out)
 
-        @pl.loop(0, levels)
-        def _(k):
+        def outputs_of(k):
             span = pl.ds(pl.multiple_of(k * particles, particles), particles)
             force_out[...] += jnp.dot(z_all[k], k_all[k], preferred_element_type=F32)
             acc = jnp.dot(s_all[span, :], g_all[...], preferred_element_type=F32)
@@ -265,15 +265,24 @@
                 y, k_all[k], (((1,), (1,)), ((), ())), preferred_element_type=F32
             )
 
-        corrected_out = f_all.at[pl.ds(0, particles)]
-        for copies in (f_copies, g_copies, geo_copies):
-            for copy in copies.values():
-                copy.wait_send()
-        corrected_out[...] = force_out[...].astype(BF16)
-        force_copy = pltpu.make_async_copy(corrected_out, corrected_ref.at[0, 0], out_sem.at[0])
-        grad_copy = pltpu.make_async_copy(grad_out, grad_ref.at[0, 0], out_sem.at[1])
-        force_copy.start()
-        grad_copy.start()
+        cuts = [0, levels * 3 // 8, levels * 6 // 8, levels]
+
+        def outputs_stage(stage):
+            pl.loop(cuts[stage], cuts[stage + 1])(outputs_of)
+
+        def send_outputs():
+            corrected_out = f_all.at[pl.ds(0, particles)]
+            for copies in (f_copies, g_copies, geo_copies):
+                for copy in copies.values():
+                    copy.wait_send()
+            corrected_out[...] = force_out[...].astype(BF16)
+            force_copy = pltpu.make_async_copy(corrected_out, corrected_ref.at[0, 0], out_sem.at[0])
+            grad_copy = pltpu.make_async_copy(grad_out, grad_ref.at[0, 0], out_sem.at[1])
+            force_copy.start()
+            grad_copy.start()
+            return force_copy, grad_copy
+
+        outputs_stage(0)
 
         total = w_part[mn].astype(F32)
         for d in range(1, nn):
@@ -308,6 +317,7 @@
             w_sum[...] = total.astype(BF16).reshape(nw, rows_w, channels)
             for d in range(1, nw):
                 scatter_copy(d).start()
+            outputs_stage(1)
             piece = w_sum[mw].astype(F32)
             for d in range(1, nw):
                 scatter_copy(d).wait_recv()
@@ -316,6 +326,8 @@
             for d in range(1, nw):
                 column_copy(d).start()
             send_row(0)
+            outputs_stage(2)
+            force_copy, grad_copy = send_outputs()
 
             @pl.loop(1, nw)
             def _(step):
@@ -343,6 +355,9 @@
             def _(d):
                 scatter_copy(d).wait()
 
+            outputs_stage(1)
+            outputs_stage(2)
+            force_copy, grad_copy = send_outputs()
             w_out[0] = (jnp.sum(w_in[...].astype(F32), axis=0) * norm).astype(BF16)
             send_row(0)
         own_copy = pltpu.make_async_copy(w_out, n_out.at[mn], out_sem.at[2])
@@ -393,20 +408,27 @@
 
 
 def deliver(
-    corrected_in, grad_in, weights_in, corrected_ref, grad_ref, weights_ref, narrow, wide, sems
+    corrected_in, grad_in, weights_in, corrected_ref, grad_ref, weights_ref,
+    corrected, grad, narrow, wide, sems,
 ):
-    load = pltpu.make_async_copy(weights_in, narrow, sems.at[0])
+    loads = [
+        pltpu.make_async_copy(weights_in, narrow, sems.at[0]),
+        pltpu.make_async_copy(grad_in, grad, sems.at[1]),
+        pltpu.make_async_copy(corrected_in, corrected, sems.at[2]),
+    ]
     copies = [
-        pltpu.make_async_copy(grad_in, grad_ref, sems.at[1]),
-        pltpu.make_async_copy(corrected_in, corrected_ref, sems.at[2]),
         pltpu.make_async_copy(wide, weights_ref, sems.at[3]),
+        pltpu.make_async_copy(grad, grad_ref, sems.at[4]),
+        pltpu.make_async_copy(corrected, corrected_ref, sems.at[5]),
     ]
-    load.start()
+    for copy in loads:
+        copy.start()
+    loads[0].wait()
+    wide[...] = narrow[...].astype(F32).reshape(wide.shape)
     copies[0].start()
-    copies[1].start()
-    load.wait()
-    wide[...] = narrow[...].astype(F32).reshape(wide.shape)
-    copies[2].start()
+    for load, copy in zip(loads[1:], copies[1:]):
+        load.wait()
+        copy.start()
     for copy in copies:
         copy.wait()
 
@@ -440,9 +462,11 @@
         in_specs=[hbm, hbm, hbm],
         out_specs=(hbm, hbm, hbm),
         scratch_shapes=[
+            pltpu.VMEM(features.shape, BF16),
+            pltpu.VMEM(features.shape, F32),
             pltpu.VMEM(gathered, BF16),
             pltpu.VMEM(kernels.shape, F32),
-            pltpu.SemaphoreType.DMA((4,)),
+            pltpu.SemaphoreType.DMA((6,)),
         ],
         compiler_params=pltpu.CompilerParams(vmem_limit_bytes=VMEM_BYTES),
         name="deliver",

time: 38.8 us -> 35.5 us (0.915)
  Pallas kernels: 37.4 us -> 34.1 us
    pallas_call x1, Pallas kernels: 4.12 us -> 1.85 us  [body(): pl.pallas_call(deliver, out_shape=outs + (jax.ShapeDtypeStruct(kernels.sh...]
    pallas_call x1, Pallas kernels: 33.3 us -> 32.2 us  [body(): pl.pallas_call(kernel, out_shape=outs + (jax.ShapeDtypeStruct(gathered, B...]
where the time goes in v1:
time: 35.5 us; the launch traced here: 35.4 us
  Pallas kernels  34.1 us (96%)
  between operations  1.28 us (4%)
    pallas_call x1, Pallas kernels, body(): pl.pallas_call(kernel, out_shape=outs + (jax.ShapeDtypeStruct(gathered, B...  32.2 us
    pallas_call x1, Pallas kernels, body(): pl.pallas_call(deliver, out_shape=outs + (jax.ShapeDtypeStruct(kernels.sh...  1.85 us

profile of v1, /device:TPU:0, one launch (start us, length us, event | category | flops | bytes accessed | tf_op | source)
XLA Modules:
  0.0 35.4 jit_solution(6437448305670253549)
XLA Ops:
  1.3 32.2 %antisymmetric_convolution.1 = (bf16[1,1,128,128]{3,2,1,0:T(8,128)(2,1)}, f32[1,1,128,128]{3,2,1,0:T(8,128)}, bf16[4,8,32,128]{3,2,1,0:T(8,128)(2,1)}) custom-call(s32[1,1]{1,0:T(1,128)S(6)} %copy.9.counts_ref, s32[1,1,8]{2,1,0:T(1,128)} %owned_ref.1, bf16[1,1,128,128]{3,2,1,0:T(8,128)(2,1)} %feat_ref.1, bf16[1,1,2,128]{3,2,1,0:T(2,128)(2,1)} %off_ref.1, ...), custom_call_target="tpu_custom_call" | custom-call | tf_op jit(solution)/shard_map/antisymmetric_convolution/pallas_call | solution.py:448
  33.5 1.8 %deliver.1 = (bf16[1,1,128,128]{3,2,1,0:T(8,128)(2,1)}, f32[1,1,128,128]{3,2,1,0:T(8,128)}, f32[8,128,128]{2,1,0:T(8,128)}) custom-call(bf16[1,1,128,128]{3,2,1,0:T(8,128)(2,1)} %get-tuple-element.6.corrected_in, f32[1,1,128,128]{3,2,1,0:T(8,128)} %get-tuple-element.7.grad_in, bf16[4,8,32,128]{3,2,1,0:T(8,128)(2,1)} %get-tuple-element.8.weights_in), custom_call_target="tpu_custom_call" | custom-call | tf_op jit(solution)/shard_map/deliver/pallas_call | solution.py:459

commit v2 on v1

--- a/solution.py
+++ b/solution.py
@@ -96,16 +96,14 @@
             geo_copies[slot] = copy
 
         def send_f(src, slot, peer):
-            copy = remote(
-                block(f_all, src), block(f_all, slot), f_send.at[slot], f_recv.at[slot], peer
-            )
+            held = block(f_all, src) if src else feat_ref.at[0, 0]
+            copy = remote(held, block(f_all, slot), f_send.at[slot], f_recv.at[slot], peer)
             copy.start()
             f_copies[slot] = copy
 
         def send_g(src, slot, peer):
-            copy = remote(
-                block(g_all, src), block(g_all, slot), g_send.at[slot], g_recv.at[slot], peer
-            )
+            held = block(g_all, src) if src else cot_ref.at[0, 0]
+            copy = remote(held, block(g_all, slot), g_send.at[slot], g_recv.at[slot], peer)
             copy.start()
             g_copies[slot] = copy
 
@@ -119,12 +117,12 @@
         own_sends += [(spot(0, -d), narrow_peer(d)) for d in (1, -1)]
         for slot, peer in own_sends:
             send_geo(0, slot, peer)
-        feat_in.wait()
         for slot, peer in own_sends:
             send_f(0, slot, peer)
-        cot_in.wait()
         for slot, peer in own_sends:
             send_g(0, slot, peer)
+        feat_in.wait()
+        cot_in.wait()
 
         own_x[...] = jnp.broadcast_to(off[0:1], (particles, particles)).T
         own_y[...] = jnp.broadcast_to(off[1:2], (particles, particles)).T
@@ -225,12 +223,15 @@
         if levels % nn == 0:
             each = levels // nn
 
-            @pl.loop(1, nn + 1)
-            def _(d):
+            turn = 1 - 2 * lax.rem(mn, 2)
+
+            @pl.loop(0, nn)
+            def _(step):
+                d = lax.rem(nn // 2 + nn + turn * step, nn)
                 piece = narrow_peer(d)[1]
                 w_part[piece] = finish_z(piece * each, each)
 
-                @pl.when(d < nn)
+                @pl.when(d > 0)
                 def _():
                     part_copy(d).start()
         else:
@@ -265,7 +266,7 @@
                 y, k_all[k], (((1,), (1,)), ((), ())), preferred_element_type=F32
             )
 
-        cuts = [0, levels * 3 // 8, levels * 6 // 8, levels]
+        cuts = [0, levels // 4, levels * 5 // 8, levels]
 
         def outputs_stage(stage):
             pl.loop(cuts[stage], cuts[stage + 1])(outputs_of)

time: 35.5 us -> 35.9 us (1.011)
  Pallas kernels: 34.1 us -> 34.5 us
    pallas_call x1, Pallas kernels: 32.2 us -> 32.6 us  [body(): pl.pallas_call(kernel, out_shape=outs + (jax.ShapeDtypeStruct(gathered, B...]
where the time goes in v2:
time: 35.9 us; the launch traced here: 35.7 us
  Pallas kernels  34.5 us (96%)
  between operations  1.28 us (4%)
    pallas_call x1, Pallas kernels, body(): pl.pallas_call(kernel, out_shape=outs + (jax.ShapeDtypeStruct(gathered, B...  32.6 us
    pallas_call x1, Pallas kernels, body(): pl.pallas_call(deliver, out_shape=outs + (jax.ShapeDtypeStruct(kernels.sh...  1.85 us

profile of v2, /device:TPU:0, one launch (start us, length us, event | category | flops | bytes accessed | tf_op | source)
XLA Modules:
  0.0 35.7 jit_solution(13064230320722899584)
XLA Ops:
  1.3 32.6 %antisymmetric_convolution.1 = (bf16[1,1,128,128]{3,2,1,0:T(8,128)(2,1)}, f32[1,1,128,128]{3,2,1,0:T(8,128)}, bf16[4,8,32,128]{3,2,1,0:T(8,128)(2,1)}) custom-call(s32[1,1]{1,0:T(1,128)S(6)} %copy.9.counts_ref, s32[1,1,8]{2,1,0:T(1,128)} %owned_ref.1, bf16[1,1,128,128]{3,2,1,0:T(8,128)(2,1)} %feat_ref.1, bf16[1,1,2,128]{3,2,1,0:T(2,128)(2,1)} %off_ref.1, ...), custom_call_target="tpu_custom_call" | custom-call | tf_op jit(solution)/shard_map/antisymmetric_convolution/pallas_call | solution.py:449
  33.9 1.8 %deliver.1 = (bf16[1,1,128,128]{3,2,1,0:T(8,128)(2,1)}, f32[1,1,128,128]{3,2,1,0:T(8,128)}, f32[8,128,128]{2,1,0:T(8,128)}) custom-call(bf16[1,1,128,128]{3,2,1,0:T(8,128)(2,1)} %get-tuple-element.6.corrected_in, f32[1,1,128,128]{3,2,1,0:T(8,128)} %get-tuple-element.7.grad_in, bf16[4,8,32,128]{3,2,1,0:T(8,128)(2,1)} %get-tuple-element.8.weights_in), custom_call_target="tpu_custom_call" | custom-call | tf_op jit(solution)/shard_map/deliver/pallas_call | solution.py:460

commit v3 on v1

--- a/solution.py
+++ b/solution.py
@@ -290,10 +290,8 @@
             total += n_in[d - 1].astype(F32)
 
         def row_copy(d, step):
-            at = lax.rem(mw - step + nw, nw) if scattered else 0
             return remote(
-                w_out.at[at], n_out.at[mn, at],
-                na_send.at[d - 1, step], na_recv.at[d - 1, step], narrow_peer(d),
+                w_out, n_out.at[mn], na_send.at[d - 1, step], na_recv.at[d - 1, step], narrow_peer(d)
             )
 
         def send_row(step):
@@ -325,14 +323,14 @@
             w_out[mw] = (piece * norm).astype(BF16)
             for d in range(1, nw):
                 column_copy(d).start()
-            send_row(0)
             outputs_stage(2)
-            force_copy, grad_copy = send_outputs()
 
             @pl.loop(1, nw)
             def _(step):
                 column_copy(step).wait_recv()
-                send_row(step)
+
+            send_row(0)
+            force_copy, grad_copy = send_outputs()
 
             @pl.loop(1, nw)
             def _(d):
@@ -367,10 +365,8 @@
         def _(d):
             part_copy(d).wait_send()
 
-        @pl.loop(0, gathered[1])
-        def _(step):
-            for d in range(1, nn):
-                row_copy(d, step).wait()
+        for d in range(1, nn):
+            row_copy(d, 0).wait()
 
         force_copy.wait()
         grad_copy.wait()
@@ -402,7 +398,7 @@
         dma((spots,)), dma((spots,)), dma((spots,)), dma((spots,)), dma((spots,)), dma((spots,)),
         dma((nn - 1,)), dma((nn - 1,)), dma((nw - 1,)), dma((nw - 1,)),
         dma((nw - 1,)), dma((nw - 1,)),
-        dma((nn - 1, gathered[1])), dma((nn - 1, gathered[1])),
+        dma((nn - 1, 1)), dma((nn - 1, 1)),
     ]
     return kernel, scratch, gathered
 

time: 35.5 us -> 34.8 us (0.980)
  Pallas kernels: 34.1 us -> 33.3 us
    pallas_call x1, Pallas kernels: 32.2 us -> 31.4 us  [body(): pl.pallas_call(kernel, out_shape=outs + (jax.ShapeDtypeStruct(gathered, B...]
where the time goes in v3:
time: 34.8 us; the launch traced here: 34.6 us
  Pallas kernels  33.3 us (96%)
  between operations  1.28 us (4%)
    pallas_call x1, Pallas kernels, body(): pl.pallas_call(kernel, out_shape=outs + (jax.ShapeDtypeStruct(gathered, B...  31.4 us
    pallas_call x1, Pallas kernels, body(): pl.pallas_call(deliver, out_shape=outs + (jax.ShapeDtypeStruct(kernels.sh...  1.85 us

profile of v3, /device:TPU:0, one launch (start us, length us, event | category | flops | bytes accessed | tf_op | source)
XLA Modules:
  0.0 34.6 jit_solution(14854019879137940632)
XLA Ops:
  1.3 31.4 %antisymmetric_convolution.1 = (bf16[1,1,128,128]{3,2,1,0:T(8,128)(2,1)}, f32[1,1,128,128]{3,2,1,0:T(8,128)}, bf16[4,8,32,128]{3,2,1,0:T(8,128)(2,1)}) custom-call(s32[1,1]{1,0:T(1,128)S(6)} %copy.9.counts_ref, s32[1,1,8]{2,1,0:T(1,128)} %owned_ref.1, bf16[1,1,128,128]{3,2,1,0:T(8,128)(2,1)} %feat_ref.1, bf16[1,1,2,128]{3,2,1,0:T(2,128)(2,1)} %off_ref.1, ...), custom_call_target="tpu_custom_call" | custom-call | tf_op jit(solution)/shard_map/antisymmetric_convolution/pallas_call | solution.py:444
  32.7 1.8 %deliver.1 = (bf16[1,1,128,128]{3,2,1,0:T(8,128)(2,1)}, f32[1,1,128,128]{3,2,1,0:T(8,128)}, f32[8,128,128]{2,1,0:T(8,128)}) custom-call(bf16[1,1,128,128]{3,2,1,0:T(8,128)(2,1)} %get-tuple-element.6.corrected_in, f32[1,1,128,128]{3,2,1,0:T(8,128)} %get-tuple-element.7.grad_in, bf16[4,8,32,128]{3,2,1,0:T(8,128)(2,1)} %get-tuple-element.8.weights_in), custom_call_target="tpu_custom_call" | custom-call | tf_op jit(solution)/shard_map/deliver/pallas_call | solution.py:455

commit v4 on v3

--- a/solution.py
+++ b/solution.py
@@ -265,7 +265,7 @@
                 y, k_all[k], (((1,), (1,)), ((), ())), preferred_element_type=F32
             )
 
-        cuts = [0, levels * 3 // 8, levels * 6 // 8, levels]
+        cuts = [0, levels // 4, levels // 2, levels]
 
         def outputs_stage(stage):
             pl.loop(cuts[stage], cuts[stage + 1])(outputs_of)
@@ -323,13 +323,13 @@
             w_out[mw] = (piece * norm).astype(BF16)
             for d in range(1, nw):
                 column_copy(d).start()
-            outputs_stage(2)
 
             @pl.loop(1, nw)
             def _(step):
                 column_copy(step).wait_recv()
 
             send_row(0)
+            outputs_stage(2)
             force_copy, grad_copy = send_outputs()
 
             @pl.loop(1, nw)

time: 34.8 us -> 34.8 us (level)
  no operation moved by 1% of the time
where the time goes in v4:
time: 34.8 us; the launch traced here: 34.6 us
  Pallas kernels  33.3 us (96%)
  between operations  1.28 us (4%)
    pallas_call x1, Pallas kernels, body(): pl.pallas_call(kernel, out_shape=outs + (jax.ShapeDtypeStruct(gathered, B...  31.4 us
    pallas_call x1, Pallas kernels, body(): pl.pallas_call(deliver, out_shape=outs + (jax.ShapeDtypeStruct(kernels.sh...  1.85 us

profile of v4, /device:TPU:0, one launch (start us, length us, event | category | flops | bytes accessed | tf_op | source)
XLA Modules:
  0.0 34.6 jit_solution(17750313975647090895)
XLA Ops:
  1.3 31.4 %antisymmetric_convolution.1 = (bf16[1,1,128,128]{3,2,1,0:T(8,128)(2,1)}, f32[1,1,128,128]{3,2,1,0:T(8,128)}, bf16[4,8,32,128]{3,2,1,0:T(8,128)(2,1)}) custom-call(s32[1,1]{1,0:T(1,128)S(6)} %copy.9.counts_ref, s32[1,1,8]{2,1,0:T(1,128)} %owned_ref.1, bf16[1,1,128,128]{3,2,1,0:T(8,128)(2,1)} %feat_ref.1, bf16[1,1,2,128]{3,2,1,0:T(2,128)(2,1)} %off_ref.1, ...), custom_call_target="tpu_custom_call" | custom-call | tf_op jit(solution)/shard_map/antisymmetric_convolution/pallas_call | solution.py:444
  32.7 1.8 %deliver.1 = (bf16[1,1,128,128]{3,2,1,0:T(8,128)(2,1)}, f32[1,1,128,128]{3,2,1,0:T(8,128)}, f32[8,128,128]{2,1,0:T(8,128)}) custom-call(bf16[1,1,128,128]{3,2,1,0:T(8,128)(2,1)} %get-tuple-element.6.corrected_in, f32[1,1,128,128]{3,2,1,0:T(8,128)} %get-tuple-element.7.grad_in, bf16[4,8,32,128]{3,2,1,0:T(8,128)(2,1)} %get-tuple-element.8.weights_in), custom_call_target="tpu_custom_call" | custom-call | tf_op jit(solution)/shard_map/deliver/pallas_call | solution.py:455
